TPU v7x, 256 devices: a whole 4x4x8 slice. The times are simulated.
256 devices in a mesh: dp: 8 (over y, core), queue: 32 (over z, x).
Axes of the slice: x: 4, y: 4, z: 8, core: 2. Of those that a mesh axis runs over, the one named last changes fastest.
Arguments:
- features: bfloat16 [131072, 1024], P(('dp', 'queue')), may hold values from -1 to 1
- weight: bfloat16 [1024, 256], replicated, may hold values from -2 to 2
- support_queue: bfloat16 [262144, 256], P('queue'), may hold values from -100 to 100
- owner_shard: int32 [131072, 1], P(('dp', 'queue')), may hold values from 0 to 31; in each aligned block of 512 rows (0 to 511, 512 to 1023, ...) at most 64 rows name the same one
- slot_row: int32 [131072], P(('dp', 'queue')), may hold values from 0 to 8191
- loss_weight: bfloat16 [131072], P(('dp', 'queue')), may hold values from 0.5 to 2
Outputs:
- grad_feats: bfloat16 [131072, 1024], P(('dp', 'queue'))
- grad_weight: float32 [1024, 256], replicated
Inputs may be any that keep to these rules, and one draw needn't show every extreme that they name: `owner_shard`: among the rows of one device no shard is named by more than 64 rows, a bound that some block reaches.
All inputs are finite; a program needn't handle non-finite values.
Results may differ from a plain program's by a relative error of at most 0.0035.
Values may be sent and summed in bfloat16 or wider, within the bound.
No kernel may reach another device: no remote copies, remote signals or barrier semaphores. Data moves between devices by JAX's collectives and lax.ppermute only.
A program may use at most 128 MiB of HBM per device.

v0:
```python
import functools
import math

import jax
import jax.numpy as jnp
from jax import lax
from jax.experimental import pallas as pl
from jax.experimental.pallas import tpu as pltpu
from jax.sharding import Mesh
from jax.sharding import PartitionSpec as P

TEMPER = 0.1
EPSILON = 1e-06
NZ, NX, NY, NC = 8, 4, 4, 2
CAP = 64
BF = jnp.bfloat16
F32 = jnp.float32
VMEM_LIMIT = 16 * 1024 * 1024
ALL_VMEM = 62 * 1024 * 1024
IN_VMEM = pl.BlockSpec(memory_space=pltpu.VMEM)
EXPONENT = math.log2(math.e) / TEMPER
QUEUE = ("z", "x")


def shift(size, by):
    return [(i, (i + by) % size) for i in range(size)]


def flip(size, mask):
    return [(i, i ^ mask) for i in range(size)]


def vmem_call(kernel, out_shape, name, limit=VMEM_LIMIT, **kw):
    return pl.pallas_call(
        kernel,
        out_shape=out_shape,
        compiler_params=pltpu.CompilerParams(vmem_limit_bytes=limit),
        name=name,
        **kw,
    )


def ranks(owner, shards):
    n = owner.shape[1]
    onehot = jnp.where(owner == lax.broadcasted_iota(jnp.int32, (shards, n), 0), 1.0, 0.0)
    above = lax.broadcasted_iota(jnp.int32, (n, n), 0) < lax.broadcasted_iota(jnp.int32, (n, n), 1)
    above = jnp.where(above, 1.0, 0.0).astype(BF)
    before = jnp.dot(onehot.astype(BF), above, preferred_element_type=F32)
    return onehot, jnp.sum(before * onehot, axis=0, keepdims=True).astype(jnp.int32)


def project(features, weight):
    projected = jnp.dot(features, weight, preferred_element_type=F32)
    inv = lax.rsqrt(jnp.sum(projected * projected, axis=1, keepdims=True) + EPSILON)
    return projected * inv, inv


def begin_kernel(
    feats_hbm,
    weight_hbm,
    owner_hbm,
    slot_hbm,
    view_ref,
    wanted_ref,
    feats_ref,
    weight_ref,
    owner_ref,
    slot_ref,
    sems,
):
    copies = [
        pltpu.make_async_copy(owner_hbm, owner_ref, sems.at[0]),
        pltpu.make_async_copy(slot_hbm, slot_ref, sems.at[1]),
        pltpu.make_async_copy(weight_hbm, weight_ref, sems.at[2]),
        pltpu.make_async_copy(feats_hbm, feats_ref, sems.at[3]),
    ]
    for copy in copies:
        copy.start()
    copies[0].wait()
    copies[1].wait()
    n = owner_ref.shape[1]
    slot = slot_ref[...]
    onehot, rank = ranks(owner_ref[...], wanted_ref.shape[0])
    chosen = jnp.where(rank == lax.broadcasted_iota(jnp.int32, (128, n), 0), 1.0, 0.0).astype(BF)
    both = (((1,), (1,)), ((), ()))
    high = (onehot * (slot >> 7).astype(F32)).astype(BF)
    low = (onehot * (slot & 127).astype(F32)).astype(BF)
    upper = lax.dot_general(high, chosen, both, preferred_element_type=F32)
    lower = lax.dot_general(low, chosen, both, preferred_element_type=F32)
    full = upper.astype(jnp.int32) * 128 + lower.astype(jnp.int32)
    wanted_ref[...] = full[:, :CAP]
    copies[2].wait()
    copies[3].wait()
    view_ref[...] = project(feats_ref[...], weight_ref[...])[0].astype(BF)


def begin(features, weight, owner, slot):
    n, width = features.shape[0], weight.shape[1]
    in_hbm = pl.BlockSpec(memory_space=pltpu.HBM)
    return vmem_call(
        begin_kernel,
        (
            jax.ShapeDtypeStruct((n, width), BF),
            jax.ShapeDtypeStruct((NZ * NX, CAP), jnp.int32),
        ),
        "begin",
        ALL_VMEM,
        in_specs=[in_hbm] * 4,
        out_specs=(IN_VMEM, IN_VMEM),
        scratch_shapes=[
            pltpu.VMEM(features.shape, BF),
            pltpu.VMEM(weight.shape, BF),
            pltpu.VMEM(owner.shape, jnp.int32),
            pltpu.VMEM(slot.shape, jnp.int32),
            pltpu.SemaphoreType.DMA((4,)),
        ],
    )(features, weight, owner, slot)


def column_of(row):
    return jnp.broadcast_to(row, (8, row.shape[1])).T[:, :1]


def pick_kernel(rows_ref, owner_ref, extra_ref, out_ref):
    n = owner_ref.shape[1]
    owner = owner_ref[...]
    places = column_of(owner * CAP + ranks(owner, rows_ref.shape[0] // CAP)[1])
    column = lax.broadcasted_iota(jnp.int32, (n, n), 1)
    total = None
    for at in range(0, rows_ref.shape[0], n):
        onehot = jnp.where(places == column + at, 1.0, 0.0).astype(BF)
        term = jnp.dot(onehot, rows_ref[at : at + n, :], preferred_element_type=F32)
        total = term if total is None else total + term
    unit = total * lax.rsqrt(jnp.sum(total * total, axis=1, keepdims=True) + EPSILON)
    out_ref[:n, :] = unit.astype(BF)
    out_ref[n:, :] = extra_ref[...]


def pick(rows, owner, extra):
    n = owner.shape[1]
    return vmem_call(
        pick_kernel,
        jax.ShapeDtypeStruct((n + extra.shape[0], rows.shape[1]), BF),
        "pick",
        in_specs=[IN_VMEM] * 3,
        out_specs=IN_VMEM,
    )(rows, owner, extra)


def exps_kernel(a_ref, *refs):
    views, (e_ref, t_ref) = refs[:NZ], refs[NZ:]
    n = t_ref.shape[1]
    a = a_ref[:n, :]
    half = n // 2

    def part(h, total):
        rows = pl.ds(pl.multiple_of(h * half, half), half)
        for k in range(NZ):
            dots = lax.dot_general(
                views[k][rows, :], a, (((1,), (1,)), ((), ())), preferred_element_type=F32
            )
            e = jnp.exp2(dots * EXPONENT)
            total = total + jnp.sum(e.reshape(half // 8, 8, n), axis=0)
            e_ref[k, rows, :] = e.astype(BF)
        return total

    total = lax.fori_loop(0, 2, part, jnp.zeros((8, n), F32))
    t_ref[...] = jnp.sum(total, axis=0, keepdims=True)


def exps(anchors, views):
    n = views[0].shape[0]
    return vmem_call(
        exps_kernel,
        (jax.ShapeDtypeStruct((NZ, n, n), BF), jax.ShapeDtypeStruct((1, n), F32)),
        "exps",
        in_specs=[IN_VMEM] * (1 + NZ),
        out_specs=(IN_VMEM, IN_VMEM),
    )(anchors, *views)


def weights_of(message_ref, n):
    w = message_ref[n : n + 16, :].astype(F32)
    return jnp.concatenate([w[k : k + 1, :] for k in range(n // w.shape[1])], axis=1)


def scale_kernel(*refs):
    anchors = refs[:NX]
    totals = refs[NX : 2 * NX]
    out_ref = refs[2 * NX]
    n = out_ref.shape[0] // NX
    for b in range(NX):
        t = None
        for k in range(NX):
            at = ((b - k) % NX) * n
            piece = totals[k][:, at : at + n]
            t = piece if t is None else t + piece
        column = column_of((1.0 / TEMPER) * weights_of(anchors[b], n) / t)
        out_ref[b * n : (b + 1) * n, :] = (anchors[b][:n, :].astype(F32) * column).astype(BF)


def scale(anchors, totals, n):
    return vmem_call(
        scale_kernel,
        jax.ShapeDtypeStruct((NX * n, anchors[0].shape[1]), BF),
        "scale",
        in_specs=[IN_VMEM] * (2 * NX),
        out_specs=IN_VMEM,
    )(*anchors, *totals)


def product(k, a_ref, parts):
    total = None
    for b, part in enumerate(parts):
        size = part.shape[2]
        term = jnp.dot(part[k], a_ref[b * size : (b + 1) * size, :], preferred_element_type=F32)
        total = term if total is None else total + term
    return total


def mix_kernel(which, a_ref, *refs):
    outs = iter(refs[NX:])
    for k in which:
        total = product(k, a_ref, refs[:NX])
        half = total.shape[0] // 2
        for h in range(2):
            out = next(outs)
            out[...] = total[h * half : (h + 1) * half].astype(out.dtype)


def mix(which, scaled, parts, dtype):
    shape = jax.ShapeDtypeStruct((parts[0].shape[1] // 2, scaled.shape[1]), dtype)
    return vmem_call(
        functools.partial(mix_kernel, which),
        (shape,) * (2 * len(which)),
        "mix",
        in_specs=[IN_VMEM] * (1 + NX),
        out_specs=(IN_VMEM,) * (2 * len(which)),
    )(scaled, *parts)


def finish_kernel(core_ref, *refs):
    halves, (*others, part_ref) = refs[:6], refs[6:]
    message_ref, feats_ref, weight_ref, grad_ref, keep_ref, send_ref = others
    n = feats_ref.shape[0]
    feats = feats_ref[...]
    unit, inv = project(feats, weight_ref[...])
    mixed = jnp.concatenate(
        [sum(halves[2 * k + h][...].astype(F32) for k in range(3)) for h in range(2)], axis=0
    )
    w = column_of((1.0 / TEMPER) * weights_of(message_ref, n))
    grad = mixed - w * message_ref[:n, :].astype(F32)
    along = jnp.sum(unit * grad, axis=1, keepdims=True)
    grad = ((grad - unit * along) * inv).astype(BF)
    grad_ref[...] = grad
    part_ref[...] = lax.dot_general(
        feats, grad, (((0,), (0,)), ((), ())), preferred_element_type=F32
    )
    half = keep_ref.shape[0]
    core = core_ref[0]
    keep_ref[...] = part_ref[pl.ds(pl.multiple_of(core * half, half), half), :]
    send_ref[...] = part_ref[pl.ds(pl.multiple_of((NC - 1 - core) * half, half), half), :]


def finish(core, ups, downs, own, message, features, weight):
    n, width = features.shape[0], weight.shape[1]
    half = jax.ShapeDtypeStruct((features.shape[1] // NC, width), F32)
    return vmem_call(
        finish_kernel,
        (jax.ShapeDtypeStruct((n, width), BF), half, half),
        "finish",
        in_specs=[pl.BlockSpec(memory_space=pltpu.SMEM)] + [IN_VMEM] * 9,
        out_specs=(IN_VMEM,) * 3,
        scratch_shapes=[pltpu.VMEM((features.shape[1], width), F32)],
    )(core.reshape(1), *own, *ups, *downs, message, features, weight)


def sum_everywhere(keep, send, core, beside):
    rows, width = keep.shape
    v = keep + lax.ppermute(send, "core", flip(NC, 1))
    many = NY * NX
    v = lax.all_to_all(v.astype(BF), ("y", "x"), 0, 0, tiled=True).astype(F32)
    v = jnp.sum(v.reshape(many, rows // many, width), axis=0)
    got = [lax.ppermute(v, "z", flip(NZ, m)) for m in (1, 2, 3)]
    v = (v + got[0]) + (got[1] + got[2])
    v = v + lax.ppermute(v, "z", flip(NZ, 4))
    v, beside = lax.optimization_barrier((v.astype(BF), beside))
    v = lax.optimization_barrier(jnp.broadcast_to(v[None], (many,) + v.shape))
    v = lax.all_to_all(v.reshape(rows, width), ("y", "x"), 0, 0, tiled=True)
    other = lax.ppermute(v, "core", flip(NC, 1))
    low, high = jnp.where(core == 0, v, other), jnp.where(core == 0, other, v)
    return jnp.concatenate([low, high], axis=0).astype(F32), beside


def local(features, weight, support_queue, owner_shard, slot_row, loss_weight):
    n = features.shape[0]
    width = weight.shape[1]

    core = lax.axis_index("core")
    owner = owner_shard.reshape(1, n)
    view_bf, wanted = begin(features, weight, owner, slot_row.reshape(1, n))
    views = {0: view_bf}
    views[7] = lax.ppermute(view_bf, "z", shift(NZ, 1))
    views[1] = lax.ppermute(view_bf, "z", shift(NZ, -1))
    asked = lax.all_to_all(wanted, QUEUE, split_axis=0, concat_axis=0, tiled=True)
    asked, views[7], views[1] = lax.optimization_barrier((asked, views[7], views[1]))
    views[6] = lax.ppermute(views[7], "z", shift(NZ, 1))
    views[2] = lax.ppermute(views[1], "z", shift(NZ, -1))
    picked = support_queue[asked]
    picked, views[6], views[2] = lax.optimization_barrier((picked, views[6], views[2]))
    views[5] = lax.ppermute(views[6], "z", shift(NZ, 1))
    views[3] = lax.ppermute(views[2], "z", shift(NZ, -1))
    views[4] = lax.ppermute(views[5], "z", shift(NZ, 1))
    views = [views[d] for d in range(NZ)]

    answered = lax.all_to_all(picked, QUEUE, split_axis=0, concat_axis=0, tiled=True)
    extra = jnp.zeros((16, width), BF).at[: n // width].set(loss_weight.reshape(n // width, width))
    message = pick(answered.reshape(NZ * NX * CAP, width), owner, extra)

    blocks = [message] + [lax.ppermute(message, "x", shift(NX, k)) for k in (1, 2, 3)]
    parts, totals = {}, {}
    for b in (0, 1, 3, 2):
        parts[b], totals[b] = exps(blocks[b], views)
    parts = [parts[b] for b in range(NX)]
    total = jnp.concatenate([totals[b] for b in range(NX)], axis=1)
    everyone = [total] + [lax.ppermute(total, "x", shift(NX, k)) for k in (1, 2, 3)]
    scaled = scale(blocks, everyone, n)

    def hop(v, by, part):
        return (lax.ppermute(v, "z", shift(NZ, by)).astype(F32) + part).astype(BF)

    far = mix((NZ // 2,), scaled, parts, BF)
    up0, up1, down0, down1 = mix((3, NZ - 3), scaled, parts, F32)
    ups, downs = [hop(far[0], 1, up0), up1.astype(BF)], [down0.astype(BF), hop(far[1], -1, down1)]
    for d in (2, 1):
        which = (d, NZ - d) if d > 1 else (d, NZ - d, 0)
        up0, up1, down0, down1, *own = mix(which, scaled, parts, F32)
        ups = [hop(ups[0], 1, up0), hop(ups[1], 1, up1)]
        downs = [hop(downs[0], -1, down0), hop(downs[1], -1, down1)]
    ups = [lax.ppermute(v, "z", shift(NZ, 1)) for v in ups]
    downs = [lax.ppermute(v, "z", shift(NZ, -1)) for v in downs]

    grad_proj, keep, send = finish(core, ups, downs, own, message, features, weight)
    grad_feats = jnp.dot(grad_proj, weight.T, preferred_element_type=F32).astype(BF)
    grad_weight, grad_feats = sum_everywhere(keep, send, core, grad_feats)
    return (grad_feats, grad_weight)


def solution(mesh):
    mesh = Mesh(mesh.devices.reshape(NY, NC, NZ, NX), ("y", "core", "z", "x"))
    views = ("y", "core", "z", "x")
    in_specs = (
        P(views, None),
        P(),
        P(QUEUE, None),
        P(views, None),
        P(views),
        P(views),
    )
    out_specs = (P(views, None), P())
    return jax.shard_map(local, mesh=mesh, in_specs=in_specs, out_specs=out_specs, check_vma=False)
```

profile of v0, /device:TPU:1, one launch (start us, length us, event | category | flops | bytes accessed | tf_op | source)
XLA Modules:
  0.0 189.4 jit_solution(2077352863456074180)
XLA Ops:
  0.6 2.7 %begin.1 = (bf16[512,256]{1,0:T(8,128)(2,1)}, s32[32,64]{1,0:T(8,128)}) custom-call(bf16[512,1024]{1,0:T(8,128)(2,1)} %refs_7_.1, bf16[1024,256]{1,0:T(8,128)(2,1)} %refs_8_.1, s32[1,512]{1,0:T(1,128)} %bitcast.16, s32[1,512]{1,0:T(1,128)} %bitcast.23), custom_call_target="tpu_custom_call" | custom-call | tf_op jit(solution)/shard_map/begin/pallas_call | solution.py:100
  3.3 2.5 %collective-permute-start = (bf16[512,256]{1,0:T(8,128)(2,1)}, bf16[512,256]{1,0:T(8,128)(2,1)S(1)}, u32[]{:S(2)}, u32[]{:S(2)}) collective-permute-start(bf16[512,256]{1,0:T(8,128)(2,1)} %get-tuple-element.52.refs_0_), channel_id=1, source_target_pairs={{0,4},{4,8},{8,12},{12,16},{16,20},{20,24},{24,28},{28,0},{1,5},{5... | collective-permute-start | bytes 786440 | tf_op jit(solution)/shard_map/ppermute | solution.py:303
  5.9 4.0 %collective-permute-start.1 = (bf16[512,256]{1,0:T(8,128)(2,1)}, bf16[512,256]{1,0:T(8,128)(2,1)S(1)}, u32[]{:S(2)}, u32[]{:S(2)}) collective-permute-start(bf16[512,256]{1,0:T(8,128)(2,1)} %get-tuple-element.52.refs_0_), channel_id=1, source_target_pairs={{0,28},{4,0},{8,4},{12,8},{16,12},{20,16},{24,20},{28,24},{1,29},{... | collective-permute-start | bytes 786440 | tf_op jit(solution)/shard_map/ppermute | solution.py:304
  9.9 16.6 %all_to_all.35 = s32[32,1,64]{2,1,0:T(1,128)S(1)} all-to-all(s32[32,1,64]{2,1,0:T(1,128)} %bitcast.22), channel_id=1, replica_groups=mesh['y'=4,'core'=2,'z'=8,'x'=4] {'z','x'}, dimensions={0} | all-to-all | bytes 16384 | tf_op jit(solution)/shard_map/all_to_all | solution.py:305
  26.8 2.3 %collective-permute-start.3 = (bf16[512,256]{1,0:T(8,128)(2,1)S(1)}, bf16[512,256]{1,0:T(8,128)(2,1)S(1)}, u32[]{:S(2)}, u32[]{:S(2)}) collective-permute-start(bf16[512,256]{1,0:T(8,128)(2,1)S(1)} %collective-permute-done.1.refs_1_), channel_id=1, source_target_pairs={{0,28},{4,0},{8,4},{12,8},{16,12},{20,16},{24,20},{28,24},{1,29},{... | collective-permute-start | bytes 786440 | tf_op jit(solution)/shard_map/ppermute | solution.py:308
  29.2 11.3 %gather_fusion = bf16[2048,256]{1,0:T(8,128)(2,1)} fusion(bf16[8192,256]{1,0:T(8,128)(2,1)} %param.10, s32[2048]{0:T(1024)S(1)} %broadcast_clamp_fusion), kind=kCustom, calls=%fused_computation | custom fusion | bytes 2105344 | tf_op jit(solution)/shard_map/gather | solution.py:309
  40.5 3.9 %all-to-all-start.1 = ((bf16[32,64,256]{2,1,0:T(8,128)(2,1)}), bf16[32,64,256]{2,1,0:T(8,128)(2,1)S(1)}, u32[]{:S(2)}, u32[]{:S(2)}) async-start(bf16[32,64,256]{2,1,0:T(8,128)(2,1)} %bitcast.18), calls=%async_computation.1 | async-start | bytes 2097152 | tf_op jit(solution)/shard_map/all_to_all | solution.py:316
  47.2 26.8 %collective-permute-done.8.refs_5_ = bf16[512,256]{1,0:T(8,128)(2,1)S(1)} collective-permute-done((bf16[512,256]{1,0:T(8,128)(2,1)S(1)}, bf16[512,256]{1,0:T(8,128)(2,1)S(1)}, u32[]{:S(2)}, u32[]{:S(2)}) %collective-permute-start.8) | collective-permute-done | bytes 262176 | tf_op jit(solution)/shard_map/ppermute | solution.py:311
  75.4 2.7 %collective-permute-start.5 = (bf16[528,256]{1,0:T(8,128)(2,1)S(1)}, bf16[528,256]{1,0:T(8,128)(2,1)S(1)}, u32[]{:S(2)}, u32[]{:S(2)}) collective-permute-start(bf16[528,256]{1,0:T(8,128)(2,1)S(1)} %pick.1.a_ref.refs_0_.refs_6_), channel_id=1, source_target_pairs={{0,2},{1,3},{2,0},{3,1},{4,6},{5,7},{6,4},{7,5},{8,10},{9,11},{10,... | collective-permute-start | bytes 811016 | tf_op jit(solution)/shard_map/ppermute | solution.py:320
  78.5 2.3 %collective-permute-start.6 = (bf16[528,256]{1,0:T(8,128)(2,1)S(1)}, bf16[528,256]{1,0:T(8,128)(2,1)S(1)}, u32[]{:S(2)}, u32[]{:S(2)}) collective-permute-start(bf16[528,256]{1,0:T(8,128)(2,1)S(1)} %pick.1.a_ref.refs_0_.refs_6_), channel_id=1, source_target_pairs={{0,3},{1,0},{2,1},{3,2},{4,7},{5,4},{6,5},{7,6},{8,11},{9,8},{10,9... | collective-permute-start | bytes 811016 | tf_op jit(solution)/shard_map/ppermute | solution.py:320
  80.8 1.6 exps.4
  82.4 1.6 exps.6
  84.0 5.5 %collective-permute-done.4.a_ref.refs_1_ = bf16[528,256]{1,0:T(8,128)(2,1)S(1)} collective-permute-done((bf16[528,256]{1,0:T(8,128)(2,1)S(1)}, bf16[528,256]{1,0:T(8,128)(2,1)S(1)}, u32[]{:S(2)}, u32[]{:S(2)}) %collective-permute-start.4) | collective-permute-done | bytes 270368 | tf_op jit(solution)/shard_map/ppermute | solution.py:320
  89.5 1.6 exps.5
  91.1 1.6 exps.7
  93.4 2.0 %collective-permute-start.11 = (f32[1,2048]{1,0:T(1,128)S(1)}, f32[1,2048]{1,0:T(1,128)S(1)}, u32[]{:S(2)}, u32[]{:S(2)}) collective-permute-start(f32[1,2048]{1,0:T(1,128)S(1)} %constant_dynamic-update-slice_fusion.refs_4_), channel_id=1, source_target_pairs={{0,2},{1,3},{2,0},{3,1},{4,6},{5,7},{6,4},{7,5},{8,10},{9,11},{10,... | collective-permute-start | bytes 24584 | tf_op jit(solution)/shard_map/ppermute | solution.py:326
  95.5 2.0 %collective-permute-start.12 = (f32[1,2048]{1,0:T(1,128)S(1)}, f32[1,2048]{1,0:T(1,128)S(1)}, u32[]{:S(2)}, u32[]{:S(2)}) collective-permute-start(f32[1,2048]{1,0:T(1,128)S(1)} %constant_dynamic-update-slice_fusion.refs_4_), channel_id=1, source_target_pairs={{0,3},{1,0},{2,1},{3,2},{4,7},{5,4},{6,5},{7,6},{8,11},{9,8},{10,9... | collective-permute-start | bytes 24584 | tf_op jit(solution)/shard_map/ppermute | solution.py:326
  99.6 2.7 %collective-permute-start.23 = (bf16[256,256]{1,0:T(8,128)(2,1)S(1)}, bf16[256,256]{1,0:T(8,128)(2,1)S(1)}, u32[]{:S(2)}, u32[]{:S(2)}) collective-permute-start(bf16[256,256]{1,0:T(8,128)(2,1)S(1)} %get-tuple-element.79), channel_id=1, source_target_pairs={{0,28},{4,0},{8,4},{12,8},{16,12},{20,16},{24,20},{28,24},{1,29},{... | collective-permute-start | bytes 393224 | tf_op jit(solution)/shard_map/ppermute | solution.py:330
  104.8 1.8 mix.4
  108.4 2.9 %collective-permute-start.24 = (bf16[256,256]{1,0:T(8,128)(2,1)S(1)}, bf16[256,256]{1,0:T(8,128)(2,1)S(1)}, u32[]{:S(2)}, u32[]{:S(2)}) collective-permute-start(bf16[256,256]{1,0:T(8,128)(2,1)S(1)} %add_convert_fusion.3), channel_id=1, source_target_pairs={{0,28},{4,0},{8,4},{12,8},{16,12},{20,16},{24,20},{28,24},{1,29},{... | collective-permute-start | bytes 393224 | tf_op jit(solution)/shard_map/ppermute | solution.py:330
  114.7 3.3 %collective-permute-start.25 = (bf16[256,256]{1,0:T(8,128)(2,1)S(1)}, bf16[256,256]{1,0:T(8,128)(2,1)S(1)}, u32[]{:S(2)}, u32[]{:S(2)}) collective-permute-start(bf16[256,256]{1,0:T(8,128)(2,1)S(1)} %add_convert_fusion.2), channel_id=1, source_target_pairs={{0,28},{4,0},{8,4},{12,8},{16,12},{20,16},{24,20},{28,24},{1,29},{... | collective-permute-start | bytes 393224 | tf_op jit(solution)/shard_map/ppermute | solution.py:330
  121.2 2.8 %collective-permute-start.26 = (bf16[256,256]{1,0:T(8,128)(2,1)S(1)}, bf16[256,256]{1,0:T(8,128)(2,1)S(1)}, u32[]{:S(2)}, u32[]{:S(2)}) collective-permute-start(bf16[256,256]{1,0:T(8,128)(2,1)S(1)} %add_convert_fusion.1), channel_id=1, source_target_pairs={{0,28},{4,0},{8,4},{12,8},{16,12},{20,16},{24,20},{28,24},{1,29},{... | collective-permute-start | bytes 393224 | tf_op jit(solution)/shard_map/ppermute | solution.py:341
  124.0 4.5 %collective-permute-done.15 = bf16[256,256]{1,0:T(8,128)(2,1)S(1)} collective-permute-done((bf16[256,256]{1,0:T(8,128)(2,1)S(1)}, bf16[256,256]{1,0:T(8,128)(2,1)S(1)}, u32[]{:S(2)}, u32[]{:S(2)}) %collective-permute-start.15) | collective-permute-done | bytes 131104 | tf_op jit(solution)/shard_map/ppermute | solution.py:330
  128.7 5.9 %collective-permute-done.16.refs_2_ = bf16[256,256]{1,0:T(8,128)(2,1)S(1)} collective-permute-done((bf16[256,256]{1,0:T(8,128)(2,1)S(1)}, bf16[256,256]{1,0:T(8,128)(2,1)S(1)}, u32[]{:S(2)}, u32[]{:S(2)}) %collective-permute-start.16) | collective-permute-done | bytes 131104 | tf_op jit(solution)/shard_map/ppermute | solution.py:340
  134.6 1.6 finish.1
  136.2 7.5 %collective-permute-start.27 = (f32[512,256]{1,0:T(8,128)S(1)}, f32[512,256]{1,0:T(8,128)S(1)}, u32[]{:S(2)}, u32[]{:S(2)}) collective-permute-start(f32[512,256]{1,0:T(8,128)S(1)} %get-tuple-element.84), channel_id=1, source_target_pairs={{0,32},{32,0},{1,33},{33,1},{2,34},{34,2},{3,35},{35,3},{4,36},{36... | collective-permute-start | bytes 1572872 | tf_op jit(solution)/shard_map/ppermute | solution.py:280
  145.3 13.6 %all_to_all.36 = bf16[16,32,256]{2,1,0:T(8,128)(2,1)S(1)} all-to-all(bf16[16,32,256]{2,1,0:T(8,128)(2,1)S(1)} %bitcast.19), channel_id=1, replica_groups=mesh['y'=4,'core'=2,'z'=8,'x'=4] {'y','x'}, dimensions={0} | all-to-all | bytes 524288 | tf_op jit(solution)/shard_map/all_to_all | solution.py:282
  159.8 2.8 %collective-permute-start.30 = (f32[32,256]{1,0:T(8,128)S(1)}, f32[32,256]{1,0:T(8,128)S(1)}, u32[]{:S(2)}, u32[]{:S(2)}) collective-permute-start(f32[32,256]{1,0:T(8,128)S(1)} %convert_reduce_fusion), channel_id=1, source_target_pairs={{0,12},{4,8},{8,4},{12,0},{16,28},{20,24},{24,20},{28,16},{1,13},{... | collective-permute-start | bytes 98312 | tf_op jit(solution)/shard_map/ppermute | solution.py:284
  164.4 3.5 %collective-permute-start.31 = (f32[32,256]{1,0:T(8,128)S(1)}, f32[32,256]{1,0:T(8,128)S(1)}, u32[]{:S(2)}, u32[]{:S(2)}) collective-permute-start(f32[32,256]{1,0:T(8,128)S(1)} %add_add_fusion), channel_id=1, source_target_pairs={{0,16},{4,20},{8,24},{12,28},{16,0},{20,4},{24,8},{28,12},{1,17},{... | collective-permute-start | bytes 98312 | tf_op jit(solution)/shard_map/ppermute | solution.py:286
  169.3 1.8 collective-permute-done.31
  171.1 10.1 %all_to_all.37 = bf16[16,32,256]{2,1,0:T(8,128)(2,1)S(1)} all-to-all(bf16[16,32,256]{2,1,0:T(8,128)(2,1)S(1)} %broadcast_in_dim.5), channel_id=1, replica_groups=mesh['y'=4,'core'=2,'z'=8,'x'=4] {'y','x'}, dimensions={0} | all-to-all | bytes 524288 | tf_op jit(solution)/shard_map/all_to_all | solution.py:289
  181.3 5.8 %collective-permute-start.32 = (bf16[512,256]{1,0:T(8,128)(2,1)S(1)}, bf16[512,256]{1,0:T(8,128)(2,1)S(1)}, u32[]{:S(2)}, u32[]{:S(2)}) collective-permute-start(bf16[512,256]{1,0:T(8,128)(2,1)S(1)} %bitcast.20), channel_id=1, source_target_pairs={{0,32},{32,0},{1,33},{33,1},{2,34},{34,2},{3,35},{35,3},{4,36},{36... | collective-permute-start | bytes 786440 | tf_op jit(solution)/shard_map/ppermute | solution.py:290
  (91 shorter events, 26.6 us)
Async XLA Ops:
  3.3 23.1 %collective-permute-start = (bf16[512,256]{1,0:T(8,128)(2,1)}, bf16[512,256]{1,0:T(8,128)(2,1)S(1)}, u32[]{:S(2)}, u32[]{:S(2)}) collective-permute-start(bf16[512,256]{1,0:T(8,128)(2,1)} %get-tuple-element.52.refs_0_), channel_id=1, source_target_pairs={{0,4},{4,8},{8,12},{12,16},{16,20},{20,24},{24,28},{28,0},{1,5},{5... | collective-permute-start | bytes 786440 | tf_op jit(solution)/shard_map/ppermute | solution.py:303
  5.9 20.6 %collective-permute-start.1 = (bf16[512,256]{1,0:T(8,128)(2,1)}, bf16[512,256]{1,0:T(8,128)(2,1)S(1)}, u32[]{:S(2)}, u32[]{:S(2)}) collective-permute-start(bf16[512,256]{1,0:T(8,128)(2,1)} %get-tuple-element.52.refs_0_), channel_id=1, source_target_pairs={{0,28},{4,0},{8,4},{12,8},{16,12},{20,16},{24,20},{28,24},{1,29},{... | collective-permute-start | bytes 786440 | tf_op jit(solution)/shard_map/ppermute | solution.py:304
  26.5 14.1 %collective-permute-start.2 = (bf16[512,256]{1,0:T(8,128)(2,1)S(1)}, bf16[512,256]{1,0:T(8,128)(2,1)S(1)}, u32[]{:S(2)}, u32[]{:S(2)}) collective-permute-start(bf16[512,256]{1,0:T(8,128)(2,1)S(1)} %collective-permute-done.refs_7_), channel_id=1, source_target_pairs={{0,4},{4,8},{8,12},{12,16},{16,20},{20,24},{24,28},{28,0},{1,5},{5... | collective-permute-start | bytes 786440 | tf_op jit(solution)/shard_map/ppermute | solution.py:307
  26.8 13.7 %collective-permute-start.3 = (bf16[512,256]{1,0:T(8,128)(2,1)S(1)}, bf16[512,256]{1,0:T(8,128)(2,1)S(1)}, u32[]{:S(2)}, u32[]{:S(2)}) collective-permute-start(bf16[512,256]{1,0:T(8,128)(2,1)S(1)} %collective-permute-done.1.refs_1_), channel_id=1, source_target_pairs={{0,28},{4,0},{8,4},{12,8},{16,12},{20,16},{24,20},{28,24},{1,29},{... | collective-permute-start | bytes 786440 | tf_op jit(solution)/shard_map/ppermute | solution.py:308
  40.5 33.6 %all-to-all-start.1 = ((bf16[32,64,256]{2,1,0:T(8,128)(2,1)}), bf16[32,64,256]{2,1,0:T(8,128)(2,1)S(1)}, u32[]{:S(2)}, u32[]{:S(2)}) async-start(bf16[32,64,256]{2,1,0:T(8,128)(2,1)} %bitcast.18), calls=%async_computation.1 | async-start | bytes 2097152 | tf_op jit(solution)/shard_map/all_to_all | solution.py:316
  44.5 29.6 %collective-permute-start.8 = (bf16[512,256]{1,0:T(8,128)(2,1)S(1)}, bf16[512,256]{1,0:T(8,128)(2,1)S(1)}, u32[]{:S(2)}, u32[]{:S(2)}) collective-permute-start(bf16[512,256]{1,0:T(8,128)(2,1)S(1)} %collective-permute-done.2.refs_6_), channel_id=1, source_target_pairs={{0,4},{4,8},{8,12},{12,16},{16,20},{20,24},{24,28},{28,0},{1,5},{5... | collective-permute-start | bytes 786440 | tf_op jit(solution)/shard_map/ppermute | solution.py:311
  45.7 35.1 %collective-permute-start.7 = (bf16[512,256]{1,0:T(8,128)(2,1)S(1)}, bf16[512,256]{1,0:T(8,128)(2,1)S(1)}, u32[]{:S(2)}, u32[]{:S(2)}) collective-permute-start(bf16[512,256]{1,0:T(8,128)(2,1)S(1)} %collective-permute-done.3.refs_2_), channel_id=1, source_target_pairs={{0,28},{4,0},{8,4},{12,8},{16,12},{20,16},{24,20},{28,24},{1,29},{... | collective-permute-start | bytes 786440 | tf_op jit(solution)/shard_map/ppermute | solution.py:312
  74.1 6.8 %collective-permute-start.9 = (bf16[512,256]{1,0:T(8,128)(2,1)S(1)}, bf16[512,256]{1,0:T(8,128)(2,1)S(1)}, u32[]{:S(2)}, u32[]{:S(2)}) collective-permute-start(bf16[512,256]{1,0:T(8,128)(2,1)S(1)} %collective-permute-done.8.refs_5_), channel_id=1, source_target_pairs={{0,4},{4,8},{8,12},{12,16},{16,20},{20,24},{24,28},{28,0},{1,5},{5... | collective-permute-start | bytes 786440 | tf_op jit(solution)/shard_map/ppermute | solution.py:313
  75.4 7.0 %collective-permute-start.5 = (bf16[528,256]{1,0:T(8,128)(2,1)S(1)}, bf16[528,256]{1,0:T(8,128)(2,1)S(1)}, u32[]{:S(2)}, u32[]{:S(2)}) collective-permute-start(bf16[528,256]{1,0:T(8,128)(2,1)S(1)} %pick.1.a_ref.refs_0_.refs_6_), channel_id=1, source_target_pairs={{0,2},{1,3},{2,0},{3,1},{4,6},{5,7},{6,4},{7,5},{8,10},{9,11},{10,... | collective-permute-start | bytes 811016 | tf_op jit(solution)/shard_map/ppermute | solution.py:320
  78.1 11.4 %collective-permute-start.4 = (bf16[528,256]{1,0:T(8,128)(2,1)S(1)}, bf16[528,256]{1,0:T(8,128)(2,1)S(1)}, u32[]{:S(2)}, u32[]{:S(2)}) collective-permute-start(bf16[528,256]{1,0:T(8,128)(2,1)S(1)} %pick.1.a_ref.refs_0_.refs_6_), channel_id=1, source_target_pairs={{0,1},{1,2},{2,3},{3,0},{4,5},{5,6},{6,7},{7,4},{8,9},{9,10},{10,1... | collective-permute-start | bytes 811016 | tf_op jit(solution)/shard_map/ppermute | solution.py:320
  78.5 12.7 %collective-permute-start.6 = (bf16[528,256]{1,0:T(8,128)(2,1)S(1)}, bf16[528,256]{1,0:T(8,128)(2,1)S(1)}, u32[]{:S(2)}, u32[]{:S(2)}) collective-permute-start(bf16[528,256]{1,0:T(8,128)(2,1)S(1)} %pick.1.a_ref.refs_0_.refs_6_), channel_id=1, source_target_pairs={{0,3},{1,0},{2,1},{3,2},{4,7},{5,4},{6,5},{7,6},{8,11},{9,8},{10,9... | collective-permute-start | bytes 811016 | tf_op jit(solution)/shard_map/ppermute | solution.py:320
  92.7 4.7 %collective-permute-start.10 = (f32[1,2048]{1,0:T(1,128)S(1)}, f32[1,2048]{1,0:T(1,128)S(1)}, u32[]{:S(2)}, u32[]{:S(2)}) collective-permute-start(f32[1,2048]{1,0:T(1,128)S(1)} %constant_dynamic-update-slice_fusion.refs_4_), channel_id=1, source_target_pairs={{0,1},{1,2},{2,3},{3,0},{4,5},{5,6},{6,7},{7,4},{8,9},{9,10},{10,1... | collective-permute-start | bytes 24584 | tf_op jit(solution)/shard_map/ppermute | solution.py:326
  93.4 4.0 %collective-permute-start.11 = (f32[1,2048]{1,0:T(1,128)S(1)}, f32[1,2048]{1,0:T(1,128)S(1)}, u32[]{:S(2)}, u32[]{:S(2)}) collective-permute-start(f32[1,2048]{1,0:T(1,128)S(1)} %constant_dynamic-update-slice_fusion.refs_4_), channel_id=1, source_target_pairs={{0,2},{1,3},{2,0},{3,1},{4,6},{5,7},{6,4},{7,5},{8,10},{9,11},{10,... | collective-permute-start | bytes 24584 | tf_op jit(solution)/shard_map/ppermute | solution.py:326
  99.6 8.8 %collective-permute-start.23 = (bf16[256,256]{1,0:T(8,128)(2,1)S(1)}, bf16[256,256]{1,0:T(8,128)(2,1)S(1)}, u32[]{:S(2)}, u32[]{:S(2)}) collective-permute-start(bf16[256,256]{1,0:T(8,128)(2,1)S(1)} %get-tuple-element.79), channel_id=1, source_target_pairs={{0,28},{4,0},{8,4},{12,8},{16,12},{20,16},{24,20},{28,24},{1,29},{... | collective-permute-start | bytes 393224 | tf_op jit(solution)/shard_map/ppermute | solution.py:330
  106.7 4.6 %collective-permute-start.20 = (bf16[256,256]{1,0:T(8,128)(2,1)S(1)}, bf16[256,256]{1,0:T(8,128)(2,1)S(1)}, u32[]{:S(2)}, u32[]{:S(2)}) collective-permute-start(bf16[256,256]{1,0:T(8,128)(2,1)S(1)} %convert_element_type.93), channel_id=1, source_target_pairs={{0,28},{4,0},{8,4},{12,8},{16,12},{20,16},{24,20},{28,24},{1,29},{... | collective-permute-start | bytes 393224 | tf_op jit(solution)/shard_map/ppermute | solution.py:330
  106.8 5.9 %collective-permute-start.17 = (bf16[256,256]{1,0:T(8,128)(2,1)S(1)}, bf16[256,256]{1,0:T(8,128)(2,1)S(1)}, u32[]{:S(2)}, u32[]{:S(2)}) collective-permute-start(bf16[256,256]{1,0:T(8,128)(2,1)S(1)} %convert_element_type.88), channel_id=1, source_target_pairs={{0,4},{4,8},{8,12},{12,16},{16,20},{20,24},{24,28},{28,0},{1,5},{5... | collective-permute-start | bytes 393224 | tf_op jit(solution)/shard_map/ppermute | solution.py:330
  108.3 5.0 %collective-permute-start.13 = (bf16[256,256]{1,0:T(8,128)(2,1)S(1)}, bf16[256,256]{1,0:T(8,128)(2,1)S(1)}, u32[]{:S(2)}, u32[]{:S(2)}) collective-permute-start(bf16[256,256]{1,0:T(8,128)(2,1)S(1)} %get-tuple-element.69), channel_id=1, source_target_pairs={{0,4},{4,8},{8,12},{12,16},{16,20},{20,24},{24,28},{28,0},{1,5},{5... | collective-permute-start | bytes 393224 | tf_op jit(solution)/shard_map/ppermute | solution.py:330
  108.4 6.2 %collective-permute-start.24 = (bf16[256,256]{1,0:T(8,128)(2,1)S(1)}, bf16[256,256]{1,0:T(8,128)(2,1)S(1)}, u32[]{:S(2)}, u32[]{:S(2)}) collective-permute-start(bf16[256,256]{1,0:T(8,128)(2,1)S(1)} %add_convert_fusion.3), channel_id=1, source_target_pairs={{0,28},{4,0},{8,4},{12,8},{16,12},{20,16},{24,20},{28,24},{1,29},{... | collective-permute-start | bytes 393224 | tf_op jit(solution)/shard_map/ppermute | solution.py:330
  111.4 6.7 %collective-permute-start.21 = (bf16[256,256]{1,0:T(8,128)(2,1)S(1)}, bf16[256,256]{1,0:T(8,128)(2,1)S(1)}, u32[]{:S(2)}, u32[]{:S(2)}) collective-permute-start(bf16[256,256]{1,0:T(8,128)(2,1)S(1)} %add_convert_fusion.5), channel_id=1, source_target_pairs={{0,28},{4,0},{8,4},{12,8},{16,12},{20,16},{24,20},{28,24},{1,29},{... | collective-permute-start | bytes 393224 | tf_op jit(solution)/shard_map/ppermute | solution.py:330
  112.8 6.8 %collective-permute-start.18 = (bf16[256,256]{1,0:T(8,128)(2,1)S(1)}, bf16[256,256]{1,0:T(8,128)(2,1)S(1)}, u32[]{:S(2)}, u32[]{:S(2)}) collective-permute-start(bf16[256,256]{1,0:T(8,128)(2,1)S(1)} %add_convert_fusion.7), channel_id=1, source_target_pairs={{0,4},{4,8},{8,12},{12,16},{16,20},{20,24},{24,28},{28,0},{1,5},{5... | collective-permute-start | bytes 393224 | tf_op jit(solution)/shard_map/ppermute | solution.py:330
  113.4 7.5 %collective-permute-start.14 = (bf16[256,256]{1,0:T(8,128)(2,1)S(1)}, bf16[256,256]{1,0:T(8,128)(2,1)S(1)}, u32[]{:S(2)}, u32[]{:S(2)}) collective-permute-start(bf16[256,256]{1,0:T(8,128)(2,1)S(1)} %add_convert_fusion.10), channel_id=1, source_target_pairs={{0,4},{4,8},{8,12},{12,16},{16,20},{20,24},{24,28},{28,0},{1,5},{5... | collective-permute-start | bytes 393224 | tf_op jit(solution)/shard_map/ppermute | solution.py:330
  114.7 6.5 %collective-permute-start.25 = (bf16[256,256]{1,0:T(8,128)(2,1)S(1)}, bf16[256,256]{1,0:T(8,128)(2,1)S(1)}, u32[]{:S(2)}, u32[]{:S(2)}) collective-permute-start(bf16[256,256]{1,0:T(8,128)(2,1)S(1)} %add_convert_fusion.2), channel_id=1, source_target_pairs={{0,28},{4,0},{8,4},{12,8},{16,12},{20,16},{24,20},{28,24},{1,29},{... | collective-permute-start | bytes 393224 | tf_op jit(solution)/shard_map/ppermute | solution.py:330
  118.0 10.6 %collective-permute-start.22 = (bf16[256,256]{1,0:T(8,128)(2,1)S(1)}, bf16[256,256]{1,0:T(8,128)(2,1)S(1)}, u32[]{:S(2)}, u32[]{:S(2)}) collective-permute-start(bf16[256,256]{1,0:T(8,128)(2,1)S(1)} %add_convert_fusion.4), channel_id=1, source_target_pairs={{0,28},{4,0},{8,4},{12,8},{16,12},{20,16},{24,20},{28,24},{1,29},{... | collective-permute-start | bytes 393224 | tf_op jit(solution)/shard_map/ppermute | solution.py:341
  119.6 9.0 %collective-permute-start.19 = (bf16[256,256]{1,0:T(8,128)(2,1)S(1)}, bf16[256,256]{1,0:T(8,128)(2,1)S(1)}, u32[]{:S(2)}, u32[]{:S(2)}) collective-permute-start(bf16[256,256]{1,0:T(8,128)(2,1)S(1)} %add_convert_fusion.6), channel_id=1, source_target_pairs={{0,4},{4,8},{8,12},{12,16},{16,20},{20,24},{24,28},{28,0},{1,5},{5... | collective-permute-start | bytes 393224 | tf_op jit(solution)/shard_map/ppermute | solution.py:340
  120.9 7.6 %collective-permute-start.15 = (bf16[256,256]{1,0:T(8,128)(2,1)S(1)}, bf16[256,256]{1,0:T(8,128)(2,1)S(1)}, u32[]{:S(2)}, u32[]{:S(2)}) collective-permute-start(bf16[256,256]{1,0:T(8,128)(2,1)S(1)} %add_convert_fusion.9), channel_id=1, source_target_pairs={{0,4},{4,8},{8,12},{12,16},{16,20},{20,24},{24,28},{28,0},{1,5},{5... | collective-permute-start | bytes 393224 | tf_op jit(solution)/shard_map/ppermute | solution.py:330
  121.2 7.5 %collective-permute-start.26 = (bf16[256,256]{1,0:T(8,128)(2,1)S(1)}, bf16[256,256]{1,0:T(8,128)(2,1)S(1)}, u32[]{:S(2)}, u32[]{:S(2)}) collective-permute-start(bf16[256,256]{1,0:T(8,128)(2,1)S(1)} %add_convert_fusion.1), channel_id=1, source_target_pairs={{0,28},{4,0},{8,4},{12,8},{16,12},{20,16},{24,20},{28,24},{1,29},{... | collective-permute-start | bytes 393224 | tf_op jit(solution)/shard_map/ppermute | solution.py:341
  128.5 6.0 %collective-permute-start.16 = (bf16[256,256]{1,0:T(8,128)(2,1)S(1)}, bf16[256,256]{1,0:T(8,128)(2,1)S(1)}, u32[]{:S(2)}, u32[]{:S(2)}) collective-permute-start(bf16[256,256]{1,0:T(8,128)(2,1)S(1)} %add_convert_fusion.8), channel_id=1, source_target_pairs={{0,4},{4,8},{8,12},{12,16},{16,20},{20,24},{24,28},{28,0},{1,5},{5... | collective-permute-start | bytes 393224 | tf_op jit(solution)/shard_map/ppermute | solution.py:340
  136.2 9.1 %collective-permute-start.27 = (f32[512,256]{1,0:T(8,128)S(1)}, f32[512,256]{1,0:T(8,128)S(1)}, u32[]{:S(2)}, u32[]{:S(2)}) collective-permute-start(f32[512,256]{1,0:T(8,128)S(1)} %get-tuple-element.84), channel_id=1, source_target_pairs={{0,32},{32,0},{1,33},{33,1},{2,34},{34,2},{3,35},{35,3},{4,36},{36... | collective-permute-start | bytes 1572872 | tf_op jit(solution)/shard_map/ppermute | solution.py:280
  159.1 3.8 %collective-permute-start.29 = (f32[32,256]{1,0:T(8,128)S(1)}, f32[32,256]{1,0:T(8,128)S(1)}, u32[]{:S(2)}, u32[]{:S(2)}) collective-permute-start(f32[32,256]{1,0:T(8,128)S(1)} %convert_reduce_fusion), channel_id=1, source_target_pairs={{0,8},{4,12},{8,0},{12,4},{16,24},{20,28},{24,16},{28,20},{1,9},{5... | collective-permute-start | bytes 98312 | tf_op jit(solution)/shard_map/ppermute | solution.py:284
  159.8 4.6 %collective-permute-start.30 = (f32[32,256]{1,0:T(8,128)S(1)}, f32[32,256]{1,0:T(8,128)S(1)}, u32[]{:S(2)}, u32[]{:S(2)}) collective-permute-start(f32[32,256]{1,0:T(8,128)S(1)} %convert_reduce_fusion), channel_id=1, source_target_pairs={{0,12},{4,8},{8,4},{12,0},{16,28},{20,24},{24,20},{28,16},{1,13},{... | collective-permute-start | bytes 98312 | tf_op jit(solution)/shard_map/ppermute | solution.py:284
  164.4 6.8 %collective-permute-start.31 = (f32[32,256]{1,0:T(8,128)S(1)}, f32[32,256]{1,0:T(8,128)S(1)}, u32[]{:S(2)}, u32[]{:S(2)}) collective-permute-start(f32[32,256]{1,0:T(8,128)S(1)} %add_add_fusion), channel_id=1, source_target_pairs={{0,16},{4,20},{8,24},{12,28},{16,0},{20,4},{24,8},{28,12},{1,17},{... | collective-permute-start | bytes 98312 | tf_op jit(solution)/shard_map/ppermute | solution.py:286
  181.3 7.0 %collective-permute-start.32 = (bf16[512,256]{1,0:T(8,128)(2,1)S(1)}, bf16[512,256]{1,0:T(8,128)(2,1)S(1)}, u32[]{:S(2)}, u32[]{:S(2)}) collective-permute-start(bf16[512,256]{1,0:T(8,128)(2,1)S(1)} %bitcast.20), channel_id=1, source_target_pairs={{0,32},{32,0},{1,33},{33,1},{2,34},{34,2},{3,35},{35,3},{4,36},{36... | collective-permute-start | bytes 786440 | tf_op jit(solution)/shard_map/ppermute | solution.py:290
  (7 other events, 203.6 us)
where the time goes:
time: 190 us; the launch traced here: 189 us
  starting transfers between devices  63.9 us (34%)
  waiting for transfers between devices  52.4 us (28%)
  blocking collectives  40.3 us (21%)
  Pallas kernels  17.5 us (9%)
  local copies, waits for them, and re-layouts  11.4 us (6%)
    ppermute x1, waiting for transfers between devices, local(): views[5] = lax.ppermute(views[6], 'z', shift(NZ, 1))  26.8 us
    all_to_all x1, blocking collectives, local(): lax.all_to_all(wanted, QUEUE, split_axis=0, concat_axis=0, tiled=True)  16.6 us
    all_to_all x1, blocking collectives, sum_everywhere(): v = lax.all_to_all(v.astype(BF), ('y', 'x'), 0, 0, tiled=True).astype(F32)  13.6 us
    ppermute x10, starting transfers between devices, hop(): return (lax.ppermute(v, 'z', shift(NZ, by)).astype(F32) + part).astype(BF)  13.1 us
    gather x1, local copies, waits for them, and re-layouts, local(): picked = support_queue[asked]  11.3 us
    all_to_all x1, blocking collectives, sum_everywhere(): v = lax.all_to_all(v.reshape(rows, width), ('y', 'x'), 0, 0, tiled=True)  10.1 us
    ppermute x1, starting transfers between devices, sum_everywhere(): v = keep + lax.ppermute(send, 'core', flip(NC, 1))  7.55 us
    ppermute x10, waiting for transfers between devices, hop(): return (lax.ppermute(v, 'z', shift(NZ, by)).astype(F32) + part).astype(BF)  7.08 us
  transfers between devices with their start and end apart: 34, of which 14 were waited for; matrix products, arithmetic and copies ran while one was open for 7% of the time, Pallas kernels for 5%

commit v1 on v0

--- a/solution.py
+++ b/solution.py
@@ -281,9 +281,9 @@
     many = NY * NX
     v = lax.all_to_all(v.astype(BF), ("y", "x"), 0, 0, tiled=True).astype(F32)
     v = jnp.sum(v.reshape(many, rows // many, width), axis=0)
-    got = [lax.ppermute(v, "z", flip(NZ, m)) for m in (1, 2, 3)]
-    v = (v + got[0]) + (got[1] + got[2])
-    v = v + lax.ppermute(v, "z", flip(NZ, 4))
+    v = lax.optimization_barrier(jnp.broadcast_to(v[None], (NZ,) + v.shape))
+    v = lax.all_to_all(v.reshape(NZ * rows // many, width), "z", 0, 0, tiled=True)
+    v = jnp.sum(v.reshape(NZ, rows // many, width), axis=0)
     v, beside = lax.optimization_barrier((v.astype(BF), beside))
     v = lax.optimization_barrier(jnp.broadcast_to(v[None], (many,) + v.shape))
     v = lax.all_to_all(v.reshape(rows, width), ("y", "x"), 0, 0, tiled=True)

time: 190 us -> 191 us (level)
  waiting for transfers between devices: 52.4 us -> 56.9 us
  starting transfers between devices: 63.9 us -> 60.2 us
    all_to_all x0 -> x1, waiting for transfers between devices: none -> 8.03 us  [sum_everywhere(): lax.all_to_all(v.reshape(NZ * rows // many, width), 'z', 0, 0, tiled=True)]
    ppermute x4 -> x0, starting transfers between devices: 7.16 us -> none  [the longest x3 3.63 us: sum_everywhere(): got = [lax.ppermute(v, 'z', flip(NZ, m)) for m in (1, 2, 3)]]
    all_to_all x0 -> x1, starting transfers between devices: none -> 4.79 us  [sum_everywhere(): lax.all_to_all(v.reshape(NZ * rows // many, width), 'z', 0, 0, tiled=True)]
    ppermute x4 -> x0, waiting for transfers between devices: 3.5 us -> none  [the longest x1 1.78 us: sum_everywhere(): v = v + lax.ppermute(v, 'z', flip(NZ, 4))]
  transfers between devices with their start and end apart: 34 -> 31, of which waited for: 14 -> 12; matrix products, arithmetic and copies ran while one was open for 7% -> 7% of each run, Pallas kernels for 5% -> 5%
where the time goes in v1:
time: 191 us
  starting transfers between devices  60.2 us (32%)
  waiting for transfers between devices  56.9 us (30%)
  blocking collectives  40.3 us (21%)
  Pallas kernels  17.5 us (9%)
  local copies, waits for them, and re-layouts  12.2 us (6%)
    ppermute x1, waiting for transfers between devices, local(): views[5] = lax.ppermute(views[6], 'z', shift(NZ, 1))  26.8 us
    all_to_all x1, blocking collectives, local(): lax.all_to_all(wanted, QUEUE, split_axis=0, concat_axis=0, tiled=True)  16.6 us
    all_to_all x1, blocking collectives, sum_everywhere(): v = lax.all_to_all(v.astype(BF), ('y', 'x'), 0, 0, tiled=True).astype(F32)  13.6 us
    ppermute x10, starting transfers between devices, hop(): return (lax.ppermute(v, 'z', shift(NZ, by)).astype(F32) + part).astype(BF)  13.1 us
    gather x1, local copies, waits for them, and re-layouts, local(): picked = support_queue[asked]  11.3 us
    all_to_all x1, blocking collectives, sum_everywhere(): v = lax.all_to_all(v.reshape(rows, width), ('y', 'x'), 0, 0, tiled=True)  10.1 us
    all_to_all x1, waiting for transfers between devices, sum_everywhere(): lax.all_to_all(v.reshape(NZ * rows // many, width), 'z', 0, 0, tiled=True)  8.03 us
    ppermute x1, starting transfers between devices, sum_everywhere(): v = keep + lax.ppermute(send, 'core', flip(NC, 1))  7.56 us
  transfers between devices with their start and end apart: 31, of which 12 were waited for; matrix products, arithmetic and copies ran while one was open for 7% of the time, Pallas kernels for 5%

profile of v1, /device:TPU:1, one launch (start us, length us, event | category | flops | bytes accessed | tf_op | source)
XLA Modules:
  0.0 191.0 jit_solution(17738651300666914029)
XLA Ops:
  0.6 2.7 %begin.1 = (bf16[512,256]{1,0:T(8,128)(2,1)}, s32[32,64]{1,0:T(8,128)}) custom-call(bf16[512,1024]{1,0:T(8,128)(2,1)} %refs_7_.1, bf16[1024,256]{1,0:T(8,128)(2,1)} %refs_8_.1, s32[1,512]{1,0:T(1,128)} %bitcast.16, s32[1,512]{1,0:T(1,128)} %bitcast.23), custom_call_target="tpu_custom_call" | custom-call | tf_op jit(solution)/shard_map/begin/pallas_call | solution.py:100
  3.3 2.5 %collective-permute-start = (bf16[512,256]{1,0:T(8,128)(2,1)}, bf16[512,256]{1,0:T(8,128)(2,1)S(1)}, u32[]{:S(2)}, u32[]{:S(2)}) collective-permute-start(bf16[512,256]{1,0:T(8,128)(2,1)} %get-tuple-element.52.refs_0_), channel_id=1, source_target_pairs={{0,4},{4,8},{8,12},{12,16},{16,20},{20,24},{24,28},{28,0},{1,5},{5... | collective-permute-start | bytes 786440 | tf_op jit(solution)/shard_map/ppermute | solution.py:303
  5.9 4.0 %collective-permute-start.1 = (bf16[512,256]{1,0:T(8,128)(2,1)}, bf16[512,256]{1,0:T(8,128)(2,1)S(1)}, u32[]{:S(2)}, u32[]{:S(2)}) collective-permute-start(bf16[512,256]{1,0:T(8,128)(2,1)} %get-tuple-element.52.refs_0_), channel_id=1, source_target_pairs={{0,28},{4,0},{8,4},{12,8},{16,12},{20,16},{24,20},{28,24},{1,29},{... | collective-permute-start | bytes 786440 | tf_op jit(solution)/shard_map/ppermute | solution.py:304
  9.9 16.6 %all_to_all.41 = s32[32,1,64]{2,1,0:T(1,128)S(1)} all-to-all(s32[32,1,64]{2,1,0:T(1,128)} %bitcast.22), channel_id=1, replica_groups=mesh['y'=4,'core'=2,'z'=8,'x'=4] {'z','x'}, dimensions={0} | all-to-all | bytes 16384 | tf_op jit(solution)/shard_map/all_to_all | solution.py:305
  26.8 2.3 %collective-permute-start.3 = (bf16[512,256]{1,0:T(8,128)(2,1)S(1)}, bf16[512,256]{1,0:T(8,128)(2,1)S(1)}, u32[]{:S(2)}, u32[]{:S(2)}) collective-permute-start(bf16[512,256]{1,0:T(8,128)(2,1)S(1)} %collective-permute-done.1.refs_1_), channel_id=1, source_target_pairs={{0,28},{4,0},{8,4},{12,8},{16,12},{20,16},{24,20},{28,24},{1,29},{... | collective-permute-start | bytes 786440 | tf_op jit(solution)/shard_map/ppermute | solution.py:308
  29.2 11.3 %gather_fusion = bf16[2048,256]{1,0:T(8,128)(2,1)} fusion(bf16[8192,256]{1,0:T(8,128)(2,1)} %param.10, s32[2048]{0:T(1024)S(1)} %broadcast_clamp_fusion), kind=kCustom, calls=%fused_computation | custom fusion | bytes 2105344 | tf_op jit(solution)/shard_map/gather | solution.py:309
  40.5 3.9 %all-to-all-start.1 = ((bf16[32,64,256]{2,1,0:T(8,128)(2,1)}), bf16[32,64,256]{2,1,0:T(8,128)(2,1)S(1)}, u32[]{:S(2)}, u32[]{:S(2)}) async-start(bf16[32,64,256]{2,1,0:T(8,128)(2,1)} %bitcast.18), calls=%async_computation.1 | async-start | bytes 2097152 | tf_op jit(solution)/shard_map/all_to_all | solution.py:316
  45.7 1.5 collective-permute-start.7
  47.2 26.8 %collective-permute-done.8.refs_5_ = bf16[512,256]{1,0:T(8,128)(2,1)S(1)} collective-permute-done((bf16[512,256]{1,0:T(8,128)(2,1)S(1)}, bf16[512,256]{1,0:T(8,128)(2,1)S(1)}, u32[]{:S(2)}, u32[]{:S(2)}) %collective-permute-start.8) | collective-permute-done | bytes 262176 | tf_op jit(solution)/shard_map/ppermute | solution.py:311
  75.4 2.7 %collective-permute-start.5 = (bf16[528,256]{1,0:T(8,128)(2,1)S(1)}, bf16[528,256]{1,0:T(8,128)(2,1)S(1)}, u32[]{:S(2)}, u32[]{:S(2)}) collective-permute-start(bf16[528,256]{1,0:T(8,128)(2,1)S(1)} %pick.1.a_ref.refs_0_.refs_6_), channel_id=1, source_target_pairs={{0,2},{1,3},{2,0},{3,1},{4,6},{5,7},{6,4},{7,5},{8,10},{9,11},{10,... | collective-permute-start | bytes 811016 | tf_op jit(solution)/shard_map/ppermute | solution.py:320
  78.5 2.3 %collective-permute-start.6 = (bf16[528,256]{1,0:T(8,128)(2,1)S(1)}, bf16[528,256]{1,0:T(8,128)(2,1)S(1)}, u32[]{:S(2)}, u32[]{:S(2)}) collective-permute-start(bf16[528,256]{1,0:T(8,128)(2,1)S(1)} %pick.1.a_ref.refs_0_.refs_6_), channel_id=1, source_target_pairs={{0,3},{1,0},{2,1},{3,2},{4,7},{5,4},{6,5},{7,6},{8,11},{9,8},{10,9... | collective-permute-start | bytes 811016 | tf_op jit(solution)/shard_map/ppermute | solution.py:320
  80.8 1.6 exps.4
  82.4 1.6 exps.6
  84.0 5.5 %collective-permute-done.4.a_ref.refs_1_ = bf16[528,256]{1,0:T(8,128)(2,1)S(1)} collective-permute-done((bf16[528,256]{1,0:T(8,128)(2,1)S(1)}, bf16[528,256]{1,0:T(8,128)(2,1)S(1)}, u32[]{:S(2)}, u32[]{:S(2)}) %collective-permute-start.4) | collective-permute-done | bytes 270368 | tf_op jit(solution)/shard_map/ppermute | solution.py:320
  89.5 1.6 exps.5
  91.1 1.6 exps.7
  93.4 2.0 %collective-permute-start.11 = (f32[1,2048]{1,0:T(1,128)S(1)}, f32[1,2048]{1,0:T(1,128)S(1)}, u32[]{:S(2)}, u32[]{:S(2)}) collective-permute-start(f32[1,2048]{1,0:T(1,128)S(1)} %constant_dynamic-update-slice_fusion.refs_4_), channel_id=1, source_target_pairs={{0,2},{1,3},{2,0},{3,1},{4,6},{5,7},{6,4},{7,5},{8,10},{9,11},{10,... | collective-permute-start | bytes 24584 | tf_op jit(solution)/shard_map/ppermute | solution.py:326
  95.4 2.0 %collective-permute-start.12 = (f32[1,2048]{1,0:T(1,128)S(1)}, f32[1,2048]{1,0:T(1,128)S(1)}, u32[]{:S(2)}, u32[]{:S(2)}) collective-permute-start(f32[1,2048]{1,0:T(1,128)S(1)} %constant_dynamic-update-slice_fusion.refs_4_), channel_id=1, source_target_pairs={{0,3},{1,0},{2,1},{3,2},{4,7},{5,4},{6,5},{7,6},{8,11},{9,8},{10,9... | collective-permute-start | bytes 24584 | tf_op jit(solution)/shard_map/ppermute | solution.py:326
  99.6 2.7 %collective-permute-start.23 = (bf16[256,256]{1,0:T(8,128)(2,1)S(1)}, bf16[256,256]{1,0:T(8,128)(2,1)S(1)}, u32[]{:S(2)}, u32[]{:S(2)}) collective-permute-start(bf16[256,256]{1,0:T(8,128)(2,1)S(1)} %get-tuple-element.79), channel_id=1, source_target_pairs={{0,28},{4,0},{8,4},{12,8},{16,12},{20,16},{24,20},{28,24},{1,29},{... | collective-permute-start | bytes 393224 | tf_op jit(solution)/shard_map/ppermute | solution.py:330
  104.8 1.8 mix.4
  108.4 2.9 %collective-permute-start.24 = (bf16[256,256]{1,0:T(8,128)(2,1)S(1)}, bf16[256,256]{1,0:T(8,128)(2,1)S(1)}, u32[]{:S(2)}, u32[]{:S(2)}) collective-permute-start(bf16[256,256]{1,0:T(8,128)(2,1)S(1)} %add_convert_fusion.3), channel_id=1, source_target_pairs={{0,28},{4,0},{8,4},{12,8},{16,12},{20,16},{24,20},{28,24},{1,29},{... | collective-permute-start | bytes 393224 | tf_op jit(solution)/shard_map/ppermute | solution.py:330
  114.7 3.4 %collective-permute-start.25 = (bf16[256,256]{1,0:T(8,128)(2,1)S(1)}, bf16[256,256]{1,0:T(8,128)(2,1)S(1)}, u32[]{:S(2)}, u32[]{:S(2)}) collective-permute-start(bf16[256,256]{1,0:T(8,128)(2,1)S(1)} %add_convert_fusion.2), channel_id=1, source_target_pairs={{0,28},{4,0},{8,4},{12,8},{16,12},{20,16},{24,20},{28,24},{1,29},{... | collective-permute-start | bytes 393224 | tf_op jit(solution)/shard_map/ppermute | solution.py:330
  121.2 2.8 %collective-permute-start.26 = (bf16[256,256]{1,0:T(8,128)(2,1)S(1)}, bf16[256,256]{1,0:T(8,128)(2,1)S(1)}, u32[]{:S(2)}, u32[]{:S(2)}) collective-permute-start(bf16[256,256]{1,0:T(8,128)(2,1)S(1)} %add_convert_fusion.1), channel_id=1, source_target_pairs={{0,28},{4,0},{8,4},{12,8},{16,12},{20,16},{24,20},{28,24},{1,29},{... | collective-permute-start | bytes 393224 | tf_op jit(solution)/shard_map/ppermute | solution.py:341
  124.0 4.5 %collective-permute-done.15 = bf16[256,256]{1,0:T(8,128)(2,1)S(1)} collective-permute-done((bf16[256,256]{1,0:T(8,128)(2,1)S(1)}, bf16[256,256]{1,0:T(8,128)(2,1)S(1)}, u32[]{:S(2)}, u32[]{:S(2)}) %collective-permute-start.15) | collective-permute-done | bytes 131104 | tf_op jit(solution)/shard_map/ppermute | solution.py:330
  128.7 5.9 %collective-permute-done.16.refs_2_ = bf16[256,256]{1,0:T(8,128)(2,1)S(1)} collective-permute-done((bf16[256,256]{1,0:T(8,128)(2,1)S(1)}, bf16[256,256]{1,0:T(8,128)(2,1)S(1)}, u32[]{:S(2)}, u32[]{:S(2)}) %collective-permute-start.16) | collective-permute-done | bytes 131104 | tf_op jit(solution)/shard_map/ppermute | solution.py:340
  134.6 1.6 finish.1
  136.2 7.6 %collective-permute-start.27 = (f32[512,256]{1,0:T(8,128)S(1)}, f32[512,256]{1,0:T(8,128)S(1)}, u32[]{:S(2)}, u32[]{:S(2)}) collective-permute-start(f32[512,256]{1,0:T(8,128)S(1)} %get-tuple-element.84), channel_id=1, source_target_pairs={{0,32},{32,0},{1,33},{33,1},{2,34},{34,2},{3,35},{35,3},{4,36},{36... | collective-permute-start | bytes 1572872 | tf_op jit(solution)/shard_map/ppermute | solution.py:280
  145.4 13.6 %all_to_all.42 = bf16[16,32,256]{2,1,0:T(8,128)(2,1)S(1)} all-to-all(bf16[16,32,256]{2,1,0:T(8,128)(2,1)S(1)} %bitcast.19), channel_id=1, replica_groups=mesh['y'=4,'core'=2,'z'=8,'x'=4] {'y','x'}, dimensions={0} | all-to-all | bytes 524288 | tf_op jit(solution)/shard_map/all_to_all | solution.py:282
  159.7 4.8 %all-to-all-start.3 = ((f32[8,32,256]{2,1,0:T(8,128)}), f32[8,32,256]{2,1,0:T(8,128)S(1)}, u32[]{:S(2)}, u32[]{:S(2)}) async-start(f32[8,32,256]{2,1,0:T(8,128)} %broadcast_in_dim.7), calls=%async_computation.3 | async-start | bytes 524288 | tf_op jit(solution)/shard_map/all_to_all | solution.py:285
  166.0 8.0 %all-to-all-done.3 = f32[8,32,256]{2,1,0:T(8,128)S(1)} async-done(((f32[8,32,256]{2,1,0:T(8,128)}), f32[8,32,256]{2,1,0:T(8,128)S(1)}, u32[]{:S(2)}, u32[]{:S(2)}) %all-to-all-start.3) | async-done | bytes 262176 | tf_op jit(solution)/shard_map/all_to_all | solution.py:285
  174.1 10.1 %all_to_all.43 = bf16[16,32,256]{2,1,0:T(8,128)(2,1)S(1)} all-to-all(bf16[16,32,256]{2,1,0:T(8,128)(2,1)S(1)} %broadcast_in_dim.8), channel_id=1, replica_groups=mesh['y'=4,'core'=2,'z'=8,'x'=4] {'y','x'}, dimensions={0} | all-to-all | bytes 524288 | tf_op jit(solution)/shard_map/all_to_all | solution.py:289
  184.2 4.6 %collective-permute-start.28 = (bf16[512,256]{1,0:T(8,128)(2,1)S(1)}, bf16[512,256]{1,0:T(8,128)(2,1)S(1)}, u32[]{:S(2)}, u32[]{:S(2)}) collective-permute-start(bf16[512,256]{1,0:T(8,128)(2,1)S(1)} %bitcast.20), channel_id=1, source_target_pairs={{0,32},{32,0},{1,33},{33,1},{2,34},{34,2},{3,35},{35,3},{4,36},{36... | collective-permute-start | bytes 786440 | tf_op jit(solution)/shard_map/ppermute | solution.py:290
  (85 shorter events, 23.2 us)
Async XLA Ops:
  3.3 23.1 %collective-permute-start = (bf16[512,256]{1,0:T(8,128)(2,1)}, bf16[512,256]{1,0:T(8,128)(2,1)S(1)}, u32[]{:S(2)}, u32[]{:S(2)}) collective-permute-start(bf16[512,256]{1,0:T(8,128)(2,1)} %get-tuple-element.52.refs_0_), channel_id=1, source_target_pairs={{0,4},{4,8},{8,12},{12,16},{16,20},{20,24},{24,28},{28,0},{1,5},{5... | collective-permute-start | bytes 786440 | tf_op jit(solution)/shard_map/ppermute | solution.py:303
  5.9 20.6 %collective-permute-start.1 = (bf16[512,256]{1,0:T(8,128)(2,1)}, bf16[512,256]{1,0:T(8,128)(2,1)S(1)}, u32[]{:S(2)}, u32[]{:S(2)}) collective-permute-start(bf16[512,256]{1,0:T(8,128)(2,1)} %get-tuple-element.52.refs_0_), channel_id=1, source_target_pairs={{0,28},{4,0},{8,4},{12,8},{16,12},{20,16},{24,20},{28,24},{1,29},{... | collective-permute-start | bytes 786440 | tf_op jit(solution)/shard_map/ppermute | solution.py:304
  26.5 14.1 %collective-permute-start.2 = (bf16[512,256]{1,0:T(8,128)(2,1)S(1)}, bf16[512,256]{1,0:T(8,128)(2,1)S(1)}, u32[]{:S(2)}, u32[]{:S(2)}) collective-permute-start(bf16[512,256]{1,0:T(8,128)(2,1)S(1)} %collective-permute-done.refs_7_), channel_id=1, source_target_pairs={{0,4},{4,8},{8,12},{12,16},{16,20},{20,24},{24,28},{28,0},{1,5},{5... | collective-permute-start | bytes 786440 | tf_op jit(solution)/shard_map/ppermute | solution.py:307
  26.8 13.7 %collective-permute-start.3 = (bf16[512,256]{1,0:T(8,128)(2,1)S(1)}, bf16[512,256]{1,0:T(8,128)(2,1)S(1)}, u32[]{:S(2)}, u32[]{:S(2)}) collective-permute-start(bf16[512,256]{1,0:T(8,128)(2,1)S(1)} %collective-permute-done.1.refs_1_), channel_id=1, source_target_pairs={{0,28},{4,0},{8,4},{12,8},{16,12},{20,16},{24,20},{28,24},{1,29},{... | collective-permute-start | bytes 786440 | tf_op jit(solution)/shard_map/ppermute | solution.py:308
  29.2 51.6 %copy-start.1 = (bf16[512,256]{1,0:T(8,128)(2,1)S(1)}, bf16[512,256]{1,0:T(8,128)(2,1)}, u32[]{:S(2)}) copy-start(bf16[512,256]{1,0:T(8,128)(2,1)} %get-tuple-element.52.refs_0_) | copy-start | bytes 786436
  40.5 33.6 %all-to-all-start.1 = ((bf16[32,64,256]{2,1,0:T(8,128)(2,1)}), bf16[32,64,256]{2,1,0:T(8,128)(2,1)S(1)}, u32[]{:S(2)}, u32[]{:S(2)}) async-start(bf16[32,64,256]{2,1,0:T(8,128)(2,1)} %bitcast.18), calls=%async_computation.1 | async-start | bytes 2097152 | tf_op jit(solution)/shard_map/all_to_all | solution.py:316
  44.5 29.6 %collective-permute-start.8 = (bf16[512,256]{1,0:T(8,128)(2,1)S(1)}, bf16[512,256]{1,0:T(8,128)(2,1)S(1)}, u32[]{:S(2)}, u32[]{:S(2)}) collective-permute-start(bf16[512,256]{1,0:T(8,128)(2,1)S(1)} %collective-permute-done.2.refs_6_), channel_id=1, source_target_pairs={{0,4},{4,8},{8,12},{12,16},{16,20},{20,24},{24,28},{28,0},{1,5},{5... | collective-permute-start | bytes 786440 | tf_op jit(solution)/shard_map/ppermute | solution.py:311
  45.7 35.1 %collective-permute-start.7 = (bf16[512,256]{1,0:T(8,128)(2,1)S(1)}, bf16[512,256]{1,0:T(8,128)(2,1)S(1)}, u32[]{:S(2)}, u32[]{:S(2)}) collective-permute-start(bf16[512,256]{1,0:T(8,128)(2,1)S(1)} %collective-permute-done.3.refs_2_), channel_id=1, source_target_pairs={{0,28},{4,0},{8,4},{12,8},{16,12},{20,16},{24,20},{28,24},{1,29},{... | collective-permute-start | bytes 786440 | tf_op jit(solution)/shard_map/ppermute | solution.py:312
  74.1 6.8 %collective-permute-start.9 = (bf16[512,256]{1,0:T(8,128)(2,1)S(1)}, bf16[512,256]{1,0:T(8,128)(2,1)S(1)}, u32[]{:S(2)}, u32[]{:S(2)}) collective-permute-start(bf16[512,256]{1,0:T(8,128)(2,1)S(1)} %collective-permute-done.8.refs_5_), channel_id=1, source_target_pairs={{0,4},{4,8},{8,12},{12,16},{16,20},{20,24},{24,28},{28,0},{1,5},{5... | collective-permute-start | bytes 786440 | tf_op jit(solution)/shard_map/ppermute | solution.py:313
  75.4 7.0 %collective-permute-start.5 = (bf16[528,256]{1,0:T(8,128)(2,1)S(1)}, bf16[528,256]{1,0:T(8,128)(2,1)S(1)}, u32[]{:S(2)}, u32[]{:S(2)}) collective-permute-start(bf16[528,256]{1,0:T(8,128)(2,1)S(1)} %pick.1.a_ref.refs_0_.refs_6_), channel_id=1, source_target_pairs={{0,2},{1,3},{2,0},{3,1},{4,6},{5,7},{6,4},{7,5},{8,10},{9,11},{10,... | collective-permute-start | bytes 811016 | tf_op jit(solution)/shard_map/ppermute | solution.py:320
  78.1 11.4 %collective-permute-start.4 = (bf16[528,256]{1,0:T(8,128)(2,1)S(1)}, bf16[528,256]{1,0:T(8,128)(2,1)S(1)}, u32[]{:S(2)}, u32[]{:S(2)}) collective-permute-start(bf16[528,256]{1,0:T(8,128)(2,1)S(1)} %pick.1.a_ref.refs_0_.refs_6_), channel_id=1, source_target_pairs={{0,1},{1,2},{2,3},{3,0},{4,5},{5,6},{6,7},{7,4},{8,9},{9,10},{10,1... | collective-permute-start | bytes 811016 | tf_op jit(solution)/shard_map/ppermute | solution.py:320
  78.5 12.7 %collective-permute-start.6 = (bf16[528,256]{1,0:T(8,128)(2,1)S(1)}, bf16[528,256]{1,0:T(8,128)(2,1)S(1)}, u32[]{:S(2)}, u32[]{:S(2)}) collective-permute-start(bf16[528,256]{1,0:T(8,128)(2,1)S(1)} %pick.1.a_ref.refs_0_.refs_6_), channel_id=1, source_target_pairs={{0,3},{1,0},{2,1},{3,2},{4,7},{5,4},{6,5},{7,6},{8,11},{9,8},{10,9... | collective-permute-start | bytes 811016 | tf_op jit(solution)/shard_map/ppermute | solution.py:320
  92.7 4.7 %collective-permute-start.10 = (f32[1,2048]{1,0:T(1,128)S(1)}, f32[1,2048]{1,0:T(1,128)S(1)}, u32[]{:S(2)}, u32[]{:S(2)}) collective-permute-start(f32[1,2048]{1,0:T(1,128)S(1)} %constant_dynamic-update-slice_fusion.refs_4_), channel_id=1, source_target_pairs={{0,1},{1,2},{2,3},{3,0},{4,5},{5,6},{6,7},{7,4},{8,9},{9,10},{10,1... | collective-permute-start | bytes 24584 | tf_op jit(solution)/shard_map/ppermute | solution.py:326
  93.4 4.0 %collective-permute-start.11 = (f32[1,2048]{1,0:T(1,128)S(1)}, f32[1,2048]{1,0:T(1,128)S(1)}, u32[]{:S(2)}, u32[]{:S(2)}) collective-permute-start(f32[1,2048]{1,0:T(1,128)S(1)} %constant_dynamic-update-slice_fusion.refs_4_), channel_id=1, source_target_pairs={{0,2},{1,3},{2,0},{3,1},{4,6},{5,7},{6,4},{7,5},{8,10},{9,11},{10,... | collective-permute-start | bytes 24584 | tf_op jit(solution)/shard_map/ppermute | solution.py:326
  95.4 2.8 %collective-permute-start.12 = (f32[1,2048]{1,0:T(1,128)S(1)}, f32[1,2048]{1,0:T(1,128)S(1)}, u32[]{:S(2)}, u32[]{:S(2)}) collective-permute-start(f32[1,2048]{1,0:T(1,128)S(1)} %constant_dynamic-update-slice_fusion.refs_4_), channel_id=1, source_target_pairs={{0,3},{1,0},{2,1},{3,2},{4,7},{5,4},{6,5},{7,6},{8,11},{9,8},{10,9... | collective-permute-start | bytes 24584 | tf_op jit(solution)/shard_map/ppermute | solution.py:326
  99.6 8.8 %collective-permute-start.23 = (bf16[256,256]{1,0:T(8,128)(2,1)S(1)}, bf16[256,256]{1,0:T(8,128)(2,1)S(1)}, u32[]{:S(2)}, u32[]{:S(2)}) collective-permute-start(bf16[256,256]{1,0:T(8,128)(2,1)S(1)} %get-tuple-element.79), channel_id=1, source_target_pairs={{0,28},{4,0},{8,4},{12,8},{16,12},{20,16},{24,20},{28,24},{1,29},{... | collective-permute-start | bytes 393224 | tf_op jit(solution)/shard_map/ppermute | solution.py:330
  106.7 4.7 %collective-permute-start.20 = (bf16[256,256]{1,0:T(8,128)(2,1)S(1)}, bf16[256,256]{1,0:T(8,128)(2,1)S(1)}, u32[]{:S(2)}, u32[]{:S(2)}) collective-permute-start(bf16[256,256]{1,0:T(8,128)(2,1)S(1)} %convert_element_type.93), channel_id=1, source_target_pairs={{0,28},{4,0},{8,4},{12,8},{16,12},{20,16},{24,20},{28,24},{1,29},{... | collective-permute-start | bytes 393224 | tf_op jit(solution)/shard_map/ppermute | solution.py:330
  106.8 5.9 %collective-permute-start.17 = (bf16[256,256]{1,0:T(8,128)(2,1)S(1)}, bf16[256,256]{1,0:T(8,128)(2,1)S(1)}, u32[]{:S(2)}, u32[]{:S(2)}) collective-permute-start(bf16[256,256]{1,0:T(8,128)(2,1)S(1)} %convert_element_type.88), channel_id=1, source_target_pairs={{0,4},{4,8},{8,12},{12,16},{16,20},{20,24},{24,28},{28,0},{1,5},{5... | collective-permute-start | bytes 393224 | tf_op jit(solution)/shard_map/ppermute | solution.py:330
  108.3 5.0 %collective-permute-start.13 = (bf16[256,256]{1,0:T(8,128)(2,1)S(1)}, bf16[256,256]{1,0:T(8,128)(2,1)S(1)}, u32[]{:S(2)}, u32[]{:S(2)}) collective-permute-start(bf16[256,256]{1,0:T(8,128)(2,1)S(1)} %get-tuple-element.69), channel_id=1, source_target_pairs={{0,4},{4,8},{8,12},{12,16},{16,20},{20,24},{24,28},{28,0},{1,5},{5... | collective-permute-start | bytes 393224 | tf_op jit(solution)/shard_map/ppermute | solution.py:330
  108.4 6.2 %collective-permute-start.24 = (bf16[256,256]{1,0:T(8,128)(2,1)S(1)}, bf16[256,256]{1,0:T(8,128)(2,1)S(1)}, u32[]{:S(2)}, u32[]{:S(2)}) collective-permute-start(bf16[256,256]{1,0:T(8,128)(2,1)S(1)} %add_convert_fusion.3), channel_id=1, source_target_pairs={{0,28},{4,0},{8,4},{12,8},{16,12},{20,16},{24,20},{28,24},{1,29},{... | collective-permute-start | bytes 393224 | tf_op jit(solution)/shard_map/ppermute | solution.py:330
  111.4 6.7 %collective-permute-start.21 = (bf16[256,256]{1,0:T(8,128)(2,1)S(1)}, bf16[256,256]{1,0:T(8,128)(2,1)S(1)}, u32[]{:S(2)}, u32[]{:S(2)}) collective-permute-start(bf16[256,256]{1,0:T(8,128)(2,1)S(1)} %add_convert_fusion.5), channel_id=1, source_target_pairs={{0,28},{4,0},{8,4},{12,8},{16,12},{20,16},{24,20},{28,24},{1,29},{... | collective-permute-start | bytes 393224 | tf_op jit(solution)/shard_map/ppermute | solution.py:330
  112.8 6.8 %collective-permute-start.18 = (bf16[256,256]{1,0:T(8,128)(2,1)S(1)}, bf16[256,256]{1,0:T(8,128)(2,1)S(1)}, u32[]{:S(2)}, u32[]{:S(2)}) collective-permute-start(bf16[256,256]{1,0:T(8,128)(2,1)S(1)} %add_convert_fusion.7), channel_id=1, source_target_pairs={{0,4},{4,8},{8,12},{12,16},{16,20},{20,24},{24,28},{28,0},{1,5},{5... | collective-permute-start | bytes 393224 | tf_op jit(solution)/shard_map/ppermute | solution.py:330
  113.4 7.5 %collective-permute-start.14 = (bf16[256,256]{1,0:T(8,128)(2,1)S(1)}, bf16[256,256]{1,0:T(8,128)(2,1)S(1)}, u32[]{:S(2)}, u32[]{:S(2)}) collective-permute-start(bf16[256,256]{1,0:T(8,128)(2,1)S(1)} %add_convert_fusion.10), channel_id=1, source_target_pairs={{0,4},{4,8},{8,12},{12,16},{16,20},{20,24},{24,28},{28,0},{1,5},{5... | collective-permute-start | bytes 393224 | tf_op jit(solution)/shard_map/ppermute | solution.py:330
  114.7 6.5 %collective-permute-start.25 = (bf16[256,256]{1,0:T(8,128)(2,1)S(1)}, bf16[256,256]{1,0:T(8,128)(2,1)S(1)}, u32[]{:S(2)}, u32[]{:S(2)}) collective-permute-start(bf16[256,256]{1,0:T(8,128)(2,1)S(1)} %add_convert_fusion.2), channel_id=1, source_target_pairs={{0,28},{4,0},{8,4},{12,8},{16,12},{20,16},{24,20},{28,24},{1,29},{... | collective-permute-start | bytes 393224 | tf_op jit(solution)/shard_map/ppermute | solution.py:330
  118.1 10.6 %collective-permute-start.22 = (bf16[256,256]{1,0:T(8,128)(2,1)S(1)}, bf16[256,256]{1,0:T(8,128)(2,1)S(1)}, u32[]{:S(2)}, u32[]{:S(2)}) collective-permute-start(bf16[256,256]{1,0:T(8,128)(2,1)S(1)} %add_convert_fusion.4), channel_id=1, source_target_pairs={{0,28},{4,0},{8,4},{12,8},{16,12},{20,16},{24,20},{28,24},{1,29},{... | collective-permute-start | bytes 393224 | tf_op jit(solution)/shard_map/ppermute | solution.py:341
  119.6 9.0 %collective-permute-start.19 = (bf16[256,256]{1,0:T(8,128)(2,1)S(1)}, bf16[256,256]{1,0:T(8,128)(2,1)S(1)}, u32[]{:S(2)}, u32[]{:S(2)}) collective-permute-start(bf16[256,256]{1,0:T(8,128)(2,1)S(1)} %add_convert_fusion.6), channel_id=1, source_target_pairs={{0,4},{4,8},{8,12},{12,16},{16,20},{20,24},{24,28},{28,0},{1,5},{5... | collective-permute-start | bytes 393224 | tf_op jit(solution)/shard_map/ppermute | solution.py:340
  120.9 7.6 %collective-permute-start.15 = (bf16[256,256]{1,0:T(8,128)(2,1)S(1)}, bf16[256,256]{1,0:T(8,128)(2,1)S(1)}, u32[]{:S(2)}, u32[]{:S(2)}) collective-permute-start(bf16[256,256]{1,0:T(8,128)(2,1)S(1)} %add_convert_fusion.9), channel_id=1, source_target_pairs={{0,4},{4,8},{8,12},{12,16},{16,20},{20,24},{24,28},{28,0},{1,5},{5... | collective-permute-start | bytes 393224 | tf_op jit(solution)/shard_map/ppermute | solution.py:330
  121.2 7.5 %collective-permute-start.26 = (bf16[256,256]{1,0:T(8,128)(2,1)S(1)}, bf16[256,256]{1,0:T(8,128)(2,1)S(1)}, u32[]{:S(2)}, u32[]{:S(2)}) collective-permute-start(bf16[256,256]{1,0:T(8,128)(2,1)S(1)} %add_convert_fusion.1), channel_id=1, source_target_pairs={{0,28},{4,0},{8,4},{12,8},{16,12},{20,16},{24,20},{28,24},{1,29},{... | collective-permute-start | bytes 393224 | tf_op jit(solution)/shard_map/ppermute | solution.py:341
  128.6 6.0 %collective-permute-start.16 = (bf16[256,256]{1,0:T(8,128)(2,1)S(1)}, bf16[256,256]{1,0:T(8,128)(2,1)S(1)}, u32[]{:S(2)}, u32[]{:S(2)}) collective-permute-start(bf16[256,256]{1,0:T(8,128)(2,1)S(1)} %add_convert_fusion.8), channel_id=1, source_target_pairs={{0,4},{4,8},{8,12},{12,16},{16,20},{20,24},{24,28},{28,0},{1,5},{5... | collective-permute-start | bytes 393224 | tf_op jit(solution)/shard_map/ppermute | solution.py:340
  136.2 9.1 %collective-permute-start.27 = (f32[512,256]{1,0:T(8,128)S(1)}, f32[512,256]{1,0:T(8,128)S(1)}, u32[]{:S(2)}, u32[]{:S(2)}) collective-permute-start(f32[512,256]{1,0:T(8,128)S(1)} %get-tuple-element.84), channel_id=1, source_target_pairs={{0,32},{32,0},{1,33},{33,1},{2,34},{34,2},{3,35},{35,3},{4,36},{36... | collective-permute-start | bytes 1572872 | tf_op jit(solution)/shard_map/ppermute | solution.py:280
  159.7 14.3 %all-to-all-start.3 = ((f32[8,32,256]{2,1,0:T(8,128)}), f32[8,32,256]{2,1,0:T(8,128)S(1)}, u32[]{:S(2)}, u32[]{:S(2)}) async-start(f32[8,32,256]{2,1,0:T(8,128)} %broadcast_in_dim.7), calls=%async_computation.3 | async-start | bytes 524288 | tf_op jit(solution)/shard_map/all_to_all | solution.py:285
  184.2 5.7 %collective-permute-start.28 = (bf16[512,256]{1,0:T(8,128)(2,1)S(1)}, bf16[512,256]{1,0:T(8,128)(2,1)S(1)}, u32[]{:S(2)}, u32[]{:S(2)}) collective-permute-start(bf16[512,256]{1,0:T(8,128)(2,1)S(1)} %bitcast.20), channel_id=1, source_target_pairs={{0,32},{32,0},{1,33},{33,1},{2,34},{34,2},{3,35},{35,3},{4,36},{36... | collective-permute-start | bytes 786440 | tf_op jit(solution)/shard_map/ppermute | solution.py:290
  (4 other events, 145.6 us)
